TPU v7x, 32 devices: a whole 2x2x4 slice. The times are simulated.
32 devices in a mesh: expert: 4 (over y, x), dp: 8 (over z, core).
Axes of the slice: x: 2, y: 2, z: 4, core: 2. Of those that a mesh axis runs over, the one named last changes fastest.
Arguments:
- tokens: bfloat16 [256, 4096], P(('expert', 'dp')), may hold values from -6 to 6
- routes: int32 [256, 2], P(('expert', 'dp')), may hold values from 0 to 3, all different within a row; in each aligned block of 8 rows (0 to 7, 8 to 15, ...) at most 6 rows name the same one
- route_weights: float32 [256, 2], P(('expert', 'dp')), may hold values from 0.2 to 1
- w_gate: bfloat16 [4, 4096, 14336], P('expert', None, 'dp'), may hold values from -0.09375 to 0.09375
- w_up: bfloat16 [4, 4096, 14336], P('expert', None, 'dp'), may hold values from -0.09375 to 0.09375
- w_down: bfloat16 [4, 14336, 4096], P('expert', 'dp'), may hold values from -0.046875 to 0.046875
Outputs:
- mixed: bfloat16 [256, 4096], P(('expert', 'dp'))
Inputs may be any that keep to these rules, and one draw needn't show every extreme that they name: `routes`: within the rows of one device (aligned blocks of 8 rows) the two experts of a token differ and no expert is named more than 6 times; in every draw some block names some expert exactly 6 times. Every expert is named somewhere.
All inputs are finite; a program needn't handle non-finite values.
Results may differ from a plain program's by a relative error of at most 0.0057.
Values may be sent and summed in bfloat16 or wider, within the bound.
A program may use at most 128 MiB of HBM per device.

v0:
```python
import jax
import jax.numpy as jnp
from jax import lax
from jax.sharding import PartitionSpec as P


def expert_projection(gate_local, up_local, down_local):

    def project(block_rows, first_row):
        gated = jnp.dot(block_rows, gate_local, preferred_element_type=jnp.float32)
        upward = jnp.dot(block_rows, up_local, preferred_element_type=jnp.float32)
        hidden = (jax.nn.silu(gated) * upward).astype(jnp.bfloat16)
        return jnp.dot(hidden, down_local, preferred_element_type=jnp.float32)

    return project


def local(tokens, routes, route_weights, w_gate, w_up, w_down):
    groups = lax.axis_size("expert")
    tok_count = tokens.shape[0]
    features = tokens.shape[1]
    capacity = 3 * tok_count // groups
    columns = groups * capacity
    listed = routes.reshape(2 * tok_count)
    chosen = (listed[:, None] == jnp.arange(groups, dtype=jnp.int32)[None, :]).astype(jnp.int32)
    before = jnp.cumsum(chosen, axis=0) - chosen
    column = listed * capacity + jnp.sum(before * chosen, axis=1)
    placing = (column[:, None] == jnp.arange(columns, dtype=jnp.int32)[None, :]).astype(
        jnp.bfloat16
    )
    placing = placing.reshape(tok_count, 2, columns)
    sending = jnp.sum(placing, axis=1)
    outgoing = jnp.einsum("tw,td->wd", sending, tokens, preferred_element_type=jnp.float32).astype(
        jnp.bfloat16
    )
    arrived = lax.all_to_all(
        outgoing.reshape(groups, capacity, features),
        "expert",
        split_axis=0,
        concat_axis=0,
        tiled=True,
    )
    arrived = arrived.reshape(columns, features)
    project = expert_projection(w_gate[0], w_up[0], w_down[0])
    partials = project(lax.all_gather(arrived, "dp", axis=0, tiled=True), jnp.int32(0))
    summed = lax.psum_scatter(partials, "dp", scatter_dimension=0, tiled=True)
    results = summed.astype(jnp.bfloat16).reshape(groups, capacity, features)
    returned = lax.all_to_all(results, "expert", split_axis=0, concat_axis=0, tiled=True).reshape(
        columns, features
    )
    picked = jnp.einsum("tkw,wd->tkd", placing, returned, preferred_element_type=jnp.float32)
    combined = jnp.sum(route_weights[:, :, None] * picked, axis=1)
    return combined.astype(jnp.bfloat16)


def solution(mesh):
    placed = (
        P(("expert", "dp"), None),
        P(("expert", "dp"), None),
        P(("expert", "dp"), None),
        P("expert", None, "dp"),
        P("expert", None, "dp"),
        P("expert", "dp", None),
    )
    return jax.shard_map(
        local, mesh=mesh, in_specs=placed, out_specs=P(("expert", "dp"), None), check_vma=False
    )
```

profile of v0, /device:TPU:0, one launch (start us, length us, event | category | flops | bytes accessed | tf_op | source)
XLA Modules:
  0.0 129.6 jit_solution(14064300226923987579)
XLA Ops:
  6.5 0.0 copy-start
  6.5 0.0 all-gather.2.cloned.1.call-start
  6.5 0.8 copy.13
  7.3 0.1 eq.51
  7.4 0.1 fusion.16
  7.5 0.2 select_reduce_fusion
  7.7 0.1 reduce_sum.33
  7.8 0.1 copy.15
  7.9 0.1 fusion.20
  8.0 0.0 copy-done
  8.0 0.3 convolution_convert_fusion
  8.2 0.1 reshape.54
  8.3 10.7 %all_to_all.10 = bf16[4,6,4096]{2,1,0:T(8,128)(2,1)S(1)} all-to-all(bf16[4,6,4096]{2,1,0:T(8,128)(2,1)S(1)} %reshape.54), channel_id=1, replica_groups=mesh['expert'=4,'dp'=8] {'expert'}, dimensions={0} | all-to-all | bytes 393216 | tf_op jit(solution)/shard_map/all_to_all | solution.py:36
  19.0 0.7 reshape.55
  19.7 0.0 all-gather.2.cloned.1.call-update
  19.8 0.0 reduce-scatter.2.cloned.1.call-start
  19.8 24.9 %all-gather.2.cloned.1.call-done = bf16[192,4096]{1,0:T(8,128)(2,1)} async-done(((bf16[24,4096]{1,0:T(8,128)(2,1)}), bf16[192,4096]{1,0:T(8,128)(2,1)}) %all-gather.2.cloned.1.call-update) | async-done | bytes 1572880 | tf_op jit(solution)/shard_map/all_gather | solution.py:45
  44.7 0.0 copy-start.2
  44.7 9.4 %fusion.4 = f32[192,1792]{1,0:T(8,128)S(1)} fusion(bf16[192,4096]{1,0:T(8,128)(2,1)} %all-gather.2.cloned.1.call-done, bf16[1,4096,1792]{2,1,0:T(8,128)(2,1)} %param.9), kind=kOutput, calls=%fused_computation.4 | convolution fusion | flops 2818572288 | bytes 17629184 | tf_op jit(solution)/shard_map/dot_general | solution.py:10
  54.1 0.0 copy-done.2
  54.1 17.4 %fusion = f32[192,4096]{1,0:T(8,128)} fusion(bf16[1,1792,4096]{2,1,0:T(8,128)(2,1)} %param.11, bf16[192,4096]{1,0:T(8,128)(2,1)S(1)} %copy-done.2, bf16[1,4096,1792]{2,1,0:T(8,128)(2,1)} %param.10, f32[192,1792]{1,0:T(8,128)S(1)} %fusion.4), kind=kOutput, calls=%fused_computation | convolution fusion | flops 5639208960 | bytes 35454976 | tf_op jit(solution)/shard_map/dot_general | solution.py:13
  71.5 0.0 reduce-scatter.2.cloned.1.call-update
  71.5 0.0 copy-start.1
  71.5 40.0 %reduce-scatter.2.cloned.1.call-done = f32[24,4096]{1,0:T(8,128)} async-done(((f32[192,4096]{1,0:T(8,128)}), f32[24,4096]{1,0:T(8,128)}) %reduce-scatter.2.cloned.1.call-update) | async-done | bytes 393232 | tf_op jit(solution)/shard_map/reduce_scatter | solution.py:46
  111.5 1.0 convert_element_type.25
  112.5 0.1 reshape.56
  112.6 9.2 %all_to_all.11 = bf16[4,6,4096]{2,1,0:T(8,128)(2,1)S(1)} all-to-all(bf16[4,6,4096]{2,1,0:T(8,128)(2,1)S(1)} %reshape.56), channel_id=1, replica_groups=mesh['expert'=4,'dp'=8] {'expert'}, dimensions={0} | all-to-all | bytes 393216 | tf_op jit(solution)/shard_map/all_to_all | solution.py:48
  121.8 0.1 reshape.58
  121.9 0.0 copy-done.1
  121.9 0.9 fusion.12
  (2 shorter events, 0.0 us)
Async XLA Ops:
  6.5 1.4 %copy-start = (bf16[8,4096]{1,0:T(8,128)(2,1)S(1)}, bf16[8,4096]{1,0:T(8,128)(2,1)}, u32[]{:S(2)}) copy-start(bf16[8,4096]{1,0:T(8,128)(2,1)} %param.6) | copy-start | bytes 196612
  6.5 38.1 %all-gather.2.cloned.1.call-start = ((), (), s32[]{:S(2)}) async-start(), calls=%async_computation.3 | async-start | bytes 1769472 | tf_op jit(solution)/shard_map/all_gather | solution.py:45
  19.8 91.8 %reduce-scatter.2.cloned.1.call-start = ((), (), s32[]{:S(2)}) async-start(), calls=%async_computation.4 | async-start | bytes 3538944 | tf_op jit(solution)/shard_map/reduce_scatter | solution.py:46
  44.7 9.4 %copy-start.2 = (bf16[192,4096]{1,0:T(8,128)(2,1)S(1)}, bf16[192,4096]{1,0:T(8,128)(2,1)}, u32[]{:S(2)}) copy-start(bf16[192,4096]{1,0:T(8,128)(2,1)} %all-gather.2.cloned.1.call-done) | copy-start | bytes 4718596
  71.5 50.4 %copy-start.1 = (f32[8,2]{0,1:T(2,128)S(1)}, f32[8,2]{0,1:T(2,128)}, u32[]{:S(2)}) copy-start(f32[8,2]{0,1:T(2,128)} %param.8) | copy-start | bytes 196
Sparse Core Ops, SparseCore 0:
  19.9 24.7 all-gather.1
  71.6 39.8 reduce-scatter.1
where the time goes:
time: 130 us
  waiting for transfers between devices  64.9 us (50%)
  matrix products  27.9 us (21%)
  blocking collectives  19.9 us (15%)
  between operations  13.5 us (10%)
  local copies, waits for them, and re-layouts  2 us (2%)
  other arithmetic  1.4 us (1%)
    reduce_scatter x1, waiting for transfers between devices, local(): summed = lax.psum_scatter(partials, 'dp', scatter_dimension=0, tiled=True)  40 us
    all_gather x1, waiting for transfers between devices, local(): lax.all_gather(arrived, 'dp', axis=0, tiled=True)  24.9 us
    dot_general x1, matrix products, project(): return jnp.dot(hidden, down_local, preferred_element_type=jnp.float32)  17.4 us
    all_to_all x1, blocking collectives, local(): lax.all_to_all(outgoing.reshape(groups, capacity, features), 'expert', sp...  10.7 us
    dot_general x1, matrix products, project(): gated = jnp.dot(block_rows, gate_local, preferred_element_type=jnp.float32)  9.36 us
    all_to_all x1, blocking collectives, local(): lax.all_to_all(results, 'expert', split_axis=0, concat_axis=0, tiled=True)  9.19 us
  transfers between devices with their start and end apart: 2, of which 2 were waited for; matrix products, arithmetic and copies ran while one was open for 0% of the time, Pallas kernels for 0%

commit v1 on v0

v1 whole, which is shorter than its diff:
```python
import functools

import jax
import jax.numpy as jnp
from jax import lax
from jax.experimental import pallas as pl
from jax.experimental.pallas import tpu as pltpu
from jax.sharding import PartitionSpec as P

MESH = pl.DeviceIdType.MESH
BF16 = jnp.bfloat16
F32 = jnp.float32
CHUNKS = 2


def tile_of(extent, most):
    return max([t for t in range(128, most + 1, 128) if extent % t == 0], default=extent)


def kernel(
    groups, ranks, capacity, block,
    tokens, routes, weights, gate_hbm, up_hbm, down_hbm, out,
    gate, up, down, w_sem,
    pair_send, pair_recv, meta, gathered,
    chosen_rows, lhs, g_acc, u_acc, hidden,
    half_send, half_recv, summed, returned, mixed_send, mixed_recv, last_send, last_recv,
    a_sem, b_sem, bm_sem, c_sem, d_sem, e_sem, f_sem, g_sem, h_sem,
):
    expert = lax.axis_index("expert")
    rank = lax.axis_index("dp")
    chips = ranks // 2
    chip, core = rank // 2, lax.rem(rank, 2)
    twin = chip * 2 + (1 - core)
    count, features = tokens.shape
    units = gate_hbm.shape[1]
    half = features // 2
    width = half // CHUNKS
    rows = groups * block
    both = 2 * count
    own_tokens = pl.ds(pl.multiple_of(chip * both, both), both)
    own_rows = pl.ds(pl.multiple_of(expert * block, block), block)

    def remote(src, dst, sems, index, where):
        return pltpu.make_async_remote_copy(
            src_ref=src, dst_ref=dst, send_sem=sems.at[(0, *index)], recv_sem=sems.at[(1, *index)],
            device_id=where, device_id_type=MESH,
        )

    to_twin = {"dp": twin}
    chip_peers = [(d, {"dp": lax.rem(chip + d, chips) * 2 + core}, lax.rem(chip + d, chips)) for d in range(1, chips)]
    expert_peers = [(d, {"expert": lax.rem(expert + d, groups)}, lax.rem(expert + d, groups)) for d in range(1, groups)]

    loads = {}
    for q in range(CHUNKS):
        for side in range(2):
            at = (core if side == 0 else 1 - core) * CHUNKS + q
            span = pl.ds(pl.multiple_of(at * width, width), width)
            loads["in", q, side] = (
                pltpu.make_async_copy(gate_hbm.at[span, :], gate.at[at], w_sem.at[0, q, side]),
                pltpu.make_async_copy(up_hbm.at[span, :], up.at[at], w_sem.at[1, q, side]),
            )
            for copy in loads["in", q, side]:
                copy.start()
    for q in range(CHUNKS):
        for side in (1, 0):
            at = (core if side == 0 else 1 - core) * CHUNKS + q
            span = pl.ds(pl.multiple_of(at * width, width), width)
            loads["out", q, side] = (pltpu.make_async_copy(down_hbm.at[:, span], down.at[at], w_sem.at[2, q, side]),)
            loads["out", q, side][0].start()

    barrier = pltpu.get_barrier_semaphore()
    pl.semaphore_signal(barrier, inc=1, device_id=to_twin, device_id_type=MESH)
    for _, where, _ in chip_peers + expert_peers:
        pl.semaphore_signal(barrier, inc=1, device_id=where, device_id_type=MESH)

    lanes = lax.broadcasted_iota(jnp.int32, (count, 128), 1)
    first, second = routes[:, 0:1], routes[:, 1:2]
    is_first = (lanes == first).astype(F32)
    is_second = (lanes == second).astype(F32)
    earlier = (
        lax.broadcasted_iota(jnp.int32, (count, count), 1) < lax.broadcasted_iota(jnp.int32, (count, count), 0)
    ).astype(F32)
    before = jnp.dot(earlier, is_first + is_second, preferred_element_type=F32)
    slot_first = jnp.sum(before * is_first, axis=1, keepdims=True)
    slot_second = jnp.sum((before + is_first) * is_second, axis=1, keepdims=True)
    base = (rank * capacity).astype(F32)
    row_first = first.astype(F32) * block + base + slot_first
    row_second = second.astype(F32) * block + base + slot_second
    facts = jnp.where(lanes == 0, row_first, 0.0)
    facts = jnp.where(lanes == 1, row_second, facts)
    facts = jnp.where(lanes == 2, weights[:, 0:1], facts)
    facts = jnp.where(lanes == 3, weights[:, 1:2], facts)
    own_facts = meta.at[pl.ds(pl.multiple_of(rank * count, count), count), :]
    own_facts[...] = facts

    everything = tokens[...].astype(F32)
    left, right = everything[:, :half], everything[:, half:]
    mine = jnp.where(core == 0, left, right)
    other = jnp.where(core == 0, right, left)
    pair_send[...] = jnp.concatenate([other[:, : half // 2], other[:, half // 2 :]], axis=0).astype(BF16)

    pl.semaphore_wait(barrier, 1 + len(chip_peers) + len(expert_peers))

    a_rows = remote(pair_send, pair_recv, a_sem, (0,), to_twin)
    a_meta = remote(own_facts, own_facts, a_sem, (1,), to_twin)
    a_rows.start()
    a_meta.start()
    a_rows.wait_recv()
    a_meta.wait_recv()
    got = pair_recv[...].astype(F32)
    theirs = jnp.concatenate([got[:count], got[count:]], axis=1)
    sixteen = jnp.concatenate(
        [jnp.where(core == 0, mine, theirs), jnp.where(core == 0, theirs, mine)], axis=0
    ).astype(BF16)

    b_copies, bm_copies = {}, []
    for d, where, _ in chip_peers:
        part = meta.at[own_tokens, :]
        bm_copies.append(remote(part, part, bm_sem, (d - 1,), where))
        bm_copies[-1].start()
    for q in range(CHUNKS):
        gathered[q, own_tokens, :] = sixteen[:, q * width : (q + 1) * width]
        for d, where, _ in chip_peers:
            part = gathered.at[q, own_tokens, :]
            b_copies[q, d] = remote(part, part, b_sem, (q, d - 1), where)
            b_copies[q, d].start()
    for copy in bm_copies:
        copy.wait_recv()
    table = meta[...]
    row_ids = lax.broadcasted_iota(jnp.int32, (ranks * count, rows), 1).astype(F32)
    pick_first = (row_ids == table[:, 0:1]).astype(BF16)
    pick_second = (row_ids == table[:, 1:2]).astype(BF16)
    picks = jnp.concatenate([pick_first, pick_second], axis=0)
    placing = pick_first + pick_second

    c_copies, d_copies = {}, {}
    for q in range(CHUNKS):
        for d, _, _ in chip_peers:
            b_copies[q, d].wait_recv()
        chosen_rows[q] = lax.dot_general(
            placing, gathered[q], (((0,), (0,)), ((), ())), preferred_element_type=F32
        ).astype(BF16)
        for d, where, there in expert_peers:
            c_copies[q, d] = remote(
                chosen_rows.at[q, pl.ds(pl.multiple_of(there * block, block), block), :],
                lhs.at[core, q, own_rows, :], c_sem, (q, d - 1), where,
            )
            c_copies[q, d].start()
        lhs[core, q, own_rows, :] = chosen_rows[q, own_rows, :]
        part = lhs.at[core, q, own_rows, :]
        d_copies[q, 0] = remote(part, part, d_sem, (q, 0), to_twin)
        d_copies[q, 0].start()

    unit_tile = tile_of(units, 512)

    def accumulate(q, side, fresh):
        at = core if side == 0 else 1 - core
        for copy in loads["in", q, side]:
            copy.wait()
        piece = at * CHUNKS + q

        def step(n, carry):
            span = pl.ds(pl.multiple_of(n * unit_tile, unit_tile), unit_tile)
            x = lhs[at, q]
            g = jnp.dot(x, gate[piece, :, span], preferred_element_type=F32)
            u = jnp.dot(x, up[piece, :, span], preferred_element_type=F32)
            if fresh:
                g_acc[:, span] = g
                u_acc[:, span] = u
            else:
                g_acc[:, span] += g
                u_acc[:, span] += u
            return carry

        lax.fori_loop(0, units // unit_tile, step, 0)

    for q in range(CHUNKS):
        for d, _, _ in expert_peers:
            c_copies[q, d].wait_recv()
            source = lax.rem(expert + groups - d, groups)
            part = lhs.at[core, q, pl.ds(pl.multiple_of(source * block, block), block), :]
            d_copies[q, d] = remote(part, part, d_sem, (q, d), to_twin)
            d_copies[q, d].start()
        accumulate(q, 0, q == 0)
        for d in range(groups):
            d_copies[q, d].wait_recv()
        accumulate(q, 1, False)

    def activate(n, carry):
        span = pl.ds(pl.multiple_of(n * unit_tile, unit_tile), unit_tile)
        g = g_acc[:, span]
        hidden[:, span] = (g / (1.0 + jnp.exp(-g)) * u_acc[:, span]).astype(BF16)
        return carry

    lax.fori_loop(0, units // unit_tile, activate, 0)

    out_tile = tile_of(width, 512)
    e_copies, f_copies = {}, {}
    for q in range(CHUNKS):
        loads["out", q, 1][0].wait()

        def foreign(n, carry):
            span = pl.ds(pl.multiple_of(n * out_tile, out_tile), out_tile)
            half_send[q, :, span] = jnp.dot(
                hidden[...], down[(1 - core) * CHUNKS + q, :, span], preferred_element_type=F32
            ).astype(BF16)
            return carry

        lax.fori_loop(0, width // out_tile, foreign, 0)
        e_copies[q] = remote(half_send.at[q], half_recv.at[q], e_sem, (q,), to_twin)
        e_copies[q].start()
        loads["out", q, 0][0].wait()
        e_copies[q].wait_recv()

        def native(n, carry):
            span = pl.ds(pl.multiple_of(n * out_tile, out_tile), out_tile)
            part = jnp.dot(hidden[...], down[core * CHUNKS + q, :, span], preferred_element_type=F32)
            summed[q, :, span] = (part + half_recv[q, :, span].astype(F32)).astype(BF16)
            return carry

        lax.fori_loop(0, width // out_tile, native, 0)
        for d, where, there in expert_peers:
            f_copies[q, d] = remote(
                summed.at[q, pl.ds(pl.multiple_of(there * block, block), block), :],
                returned.at[q, own_rows, :], f_sem, (q, d - 1), where,
            )
            f_copies[q, d].start()
        returned[q, own_rows, :] = summed[q, own_rows, :]

    g_copies = {}
    for q in range(CHUNKS):
        for d, _, _ in expert_peers:
            f_copies[q, d].wait_recv()
        picked = jnp.dot(picks, returned[q], preferred_element_type=F32)
        half_count = ranks * count
        mixture = table[:, 2:3] * picked[:half_count] + table[:, 3:4] * picked[half_count:]
        mixed_send[q] = mixture.astype(BF16)
        for d, where, there in chip_peers:
            g_copies[q, d] = remote(
                mixed_send.at[q, pl.ds(pl.multiple_of(there * both, both), both), :],
                mixed_recv.at[q, own_tokens, :], g_sem, (q, d - 1), where,
            )
            g_copies[q, d].start()
        mixed_recv[q, own_tokens, :] = mixed_send[q, own_tokens, :]

    h_copies = {}
    for q in range(CHUNKS):
        for d, _, _ in chip_peers:
            g_copies[q, d].wait_recv()
        total = mixed_recv[q, 0:both, :].astype(F32)
        for z in range(1, chips):
            total = total + mixed_recv[q, z * both : (z + 1) * both, :].astype(F32)
        low, high = total[:count], total[count:]
        keep = jnp.where(core == 0, low, high)
        give = jnp.where(core == 0, high, low)
        last_send[q] = jnp.concatenate([give[:, : width // 2], give[:, width // 2 :]], axis=0).astype(BF16)
        h_copies[q] = remote(last_send.at[q], last_recv.at[q], h_sem, (q,), to_twin)
        h_copies[q].start()
        out[:, pl.ds(pl.multiple_of(core * half + q * width, width), width)] = keep.astype(BF16)
    for q in range(CHUNKS):
        h_copies[q].wait_recv()
        got = last_recv[q].astype(F32)
        joined = jnp.concatenate([got[:count], got[count:]], axis=1)
        out[:, pl.ds(pl.multiple_of((1 - core) * half + q * width, width), width)] = joined.astype(BF16)

    sent = [a_rows, a_meta, *bm_copies]
    for copies in (b_copies, c_copies, d_copies, e_copies, f_copies, g_copies, h_copies):
        sent.extend(copies.values())
    for copy in sent:
        copy.wait_send()


def local(tokens, routes, route_weights, w_gate, w_up, w_down):
    groups, ranks = lax.axis_size("expert"), lax.axis_size("dp")
    count, features = tokens.shape
    units = w_gate.shape[2]
    capacity = 3 * count // groups
    block = -(-(ranks * capacity) // 16) * 16
    rows = groups * block
    half = features // 2
    width = half // CHUNKS
    chips = ranks // 2
    dma = pltpu.SemaphoreType.DMA
    return pl.pallas_call(
        functools.partial(kernel, groups, ranks, capacity, block),
        out_shape=jax.ShapeDtypeStruct((count, features), BF16),
        in_specs=[pl.BlockSpec(memory_space=pltpu.VMEM)] * 3 + [pl.BlockSpec(memory_space=pl.ANY)] * 3,
        out_specs=pl.BlockSpec(memory_space=pltpu.VMEM),
        scratch_shapes=[
            pltpu.VMEM((2 * CHUNKS, width, units), BF16),
            pltpu.VMEM((2 * CHUNKS, width, units), BF16),
            pltpu.VMEM((2 * CHUNKS, units, width), BF16),
            dma((3, CHUNKS, 2)),
            pltpu.VMEM((2 * count, half // 2), BF16),
            pltpu.VMEM((2 * count, half // 2), BF16),
            pltpu.VMEM((ranks * count, 128), F32),
            pltpu.VMEM((CHUNKS, ranks * count, width), BF16),
            pltpu.VMEM((CHUNKS, rows, width), BF16),
            pltpu.VMEM((2, CHUNKS, rows, width), BF16),
            pltpu.VMEM((rows, units), F32),
            pltpu.VMEM((rows, units), F32),
            pltpu.VMEM((rows, units), BF16),
            pltpu.VMEM((CHUNKS, rows, width), BF16),
            pltpu.VMEM((CHUNKS, rows, width), BF16),
            pltpu.VMEM((CHUNKS, rows, width), BF16),
            pltpu.VMEM((CHUNKS, rows, width), BF16),
            pltpu.VMEM((CHUNKS, ranks * count, width), BF16),
            pltpu.VMEM((CHUNKS, ranks * count, width), BF16),
            pltpu.VMEM((CHUNKS, 2 * count, width // 2), BF16),
            pltpu.VMEM((CHUNKS, 2 * count, width // 2), BF16),
            dma((2, 2)),
            dma((2, CHUNKS, chips - 1)),
            dma((2, chips - 1)),
            dma((2, CHUNKS, groups - 1)),
            dma((2, CHUNKS, groups)),
            dma((2, CHUNKS)),
            dma((2, CHUNKS, groups - 1)),
            dma((2, CHUNKS, chips - 1)),
            dma((2, CHUNKS)),
        ],
        compiler_params=pltpu.CompilerParams(
            collective_id=0, has_side_effects=True, vmem_limit_bytes=60 * 1024 * 1024
        ),
        cost_estimate=pl.CostEstimate(
            flops=6 * rows * features * units, bytes_accessed=6 * features * units, transcendentals=rows * units
        ),
    )(tokens, routes, route_weights, w_gate[0], w_up[0], w_down[0])


def solution(mesh):
    placed = (
        P(("expert", "dp"), None),
        P(("expert", "dp"), None),
        P(("expert", "dp"), None),
        P("expert", None, "dp"),
        P("expert", None, "dp"),
        P("expert", "dp", None),
    )
    return jax.shard_map(
        local, mesh=mesh, in_specs=placed, out_specs=P(("expert", "dp"), None), check_vma=False
    )
```

time: 130 us -> 56.1 us (0.43)
  waiting for transfers between devices: 64.9 us -> 0 us
  Pallas kernels: 0 us -> 51.7 us
  matrix products: 27.9 us -> 0 us
  blocking collectives: 19.9 us -> 0 us
  between operations: 13.5 us -> 0.01 us
  local copies, waits for them, and re-layouts: 2 us -> 4.16 us
  other arithmetic: 1.4 us -> 0 us
    pallas_call x0 -> x1, Pallas kernels: none -> 51.7 us  [local(): pl.pallas_call(functools.partial(kernel, groups, ranks, capacity, block),...]
    reduce_scatter x1 -> x0, waiting for transfers between devices: 40 us -> none  [local(): summed = lax.psum_scatter(partials, 'dp', scatter_dimension=0, tiled=True)]
    dot_general x4 -> x0, matrix products: 27.9 us -> none  [the longest x1 17.4 us: project(): return jnp.dot(hidden, down_local, preferred_element_type=jnp.float32)]
    all_gather x1 -> x0, waiting for transfers between devices: 24.9 us -> none  [local(): lax.all_gather(arrived, 'dp', axis=0, tiled=True)]
    all_to_all x2 -> x0, blocking collectives: 19.9 us -> none  [the longest x1 10.7 us: local(): lax.all_to_all(outgoing.reshape(groups, capacity, features), 'expert', sp...]
    unnamed x7 -> x3, local copies, waits for them, and re-layouts: 0.8 us -> 4.16 us
  transfers between devices with their start and end apart: 2 -> 0, of which waited for: 2 -> 0; matrix products, arithmetic and copies ran while one was open for 0% -> 0% of each run, Pallas kernels for 0% -> 0%
where the time goes in v1:
time: 56.1 us; the launch traced here: 55.9 us
  Pallas kernels  51.7 us (92%)
  local copies, waits for them, and re-layouts  4.16 us (7%)
    pallas_call x1, Pallas kernels, local(): pl.pallas_call(functools.partial(kernel, groups, ranks, capacity, block),...  51.7 us
    unnamed x3, local copies, waits for them, and re-layouts  4.16 us

profile of v1, /device:TPU:0, one launch (start us, length us, event | category | flops | bytes accessed | tf_op | source)
XLA Modules:
  0.0 55.9 jit_solution(6547385423266850618)
XLA Ops:
  0.0 1.3 %copy.7.routes = s32[8,2]{1,0:T(8,128)} copy(s32[8,2]{0,1:T(2,128)} %param.7) | data formatting | bytes 128 | tf_op args[1]
  1.3 1.3 %copy.8.weights = f32[8,2]{1,0:T(8,128)} copy(f32[8,2]{0,1:T(2,128)} %param.8) | data formatting | bytes 128 | tf_op args[2]
  2.7 51.7 %shard_map.64 = bf16[8,4096]{1,0:T(8,128)(2,1)} custom-call(bf16[8,4096]{1,0:T(8,128)(2,1)} %tokens.1, s32[8,2]{1,0:T(8,128)} %copy.7.routes, f32[8,2]{1,0:T(8,128)} %copy.8.weights, bf16[4096,1792]{1,0:T(8,128)(2,1)} %bitcast.3, bf16[4096,1792]{1,0:T(8,128)(2,1)} %bitcast.4, bf16[1792,4096]{1,0:T(8,128)(2,1)} %bitcast.5), custom_call_target="tpu_custom_call" | custom-call | flops 8455716864 | bytes 44040192 | tf_op jit(solution)/shard_map/pallas_call | solution.py:284
  54.4 1.5 %copy.10 = bf16[8,4096]{1,0:T(8,128)(2,1)} copy(bf16[8,4096]{1,0:T(8,128)(2,1)} %shard_map.64) | data formatting | bytes 131072

commit v2 on v1

v2 whole, which is shorter than its diff:
```python
import functools

import jax
import jax.numpy as jnp
from jax import lax
from jax.experimental import pallas as pl
from jax.experimental.pallas import tpu as pltpu
from jax.sharding import PartitionSpec as P

MESH = pl.DeviceIdType.MESH
BF16 = jnp.bfloat16
F32 = jnp.float32
CHUNKS = 4


def tile_of(extent, most):
    return max([t for t in range(128, most + 1, 128) if extent % t == 0], default=extent)


def kernel(
    groups, ranks, capacity, block,
    tokens, routes, weights, gate_hbm, up_hbm, down_hbm, out,
    gate, up, down, w_sem,
    folded, meta, gathered, chosen_rows, lhs, g_acc, u_acc, hidden,
    half_send, half_recv, summed, returned, mixed_send, mixed_recv,
    b_sem, bm_sem, c_sem, d_sem, e_sem, f_sem, g_sem,
):
    expert = lax.axis_index("expert")
    rank = lax.axis_index("dp")
    core = lax.rem(rank, 2)
    twin = rank + 1 - 2 * core
    count, features = tokens.shape
    units = gate_hbm.shape[1]
    half = features // 2
    width = half // CHUNKS
    fold = width // 2
    rows = groups * block
    both = 2 * count

    def rank_rows(r):
        return pl.ds(pl.multiple_of(r * both, both), both)

    def block_rows(e):
        return pl.ds(pl.multiple_of(e * block, block), block)

    def remote(src, dst, sems, index, where):
        return pltpu.make_async_remote_copy(
            src_ref=src, dst_ref=dst, send_sem=sems.at[(0, *index)], recv_sem=sems.at[(1, *index)],
            device_id=where, device_id_type=MESH,
        )

    to_twin = {"dp": twin}
    rank_peers = [(d, {"dp": lax.rem(rank + d, ranks)}, lax.rem(rank + d, ranks)) for d in range(1, ranks)]
    expert_peers = [(d, {"expert": lax.rem(expert + d, groups)}, lax.rem(expert + d, groups)) for d in range(1, groups)]

    barrier = pltpu.get_barrier_semaphore()
    for _, where, _ in rank_peers + expert_peers:
        pl.semaphore_signal(barrier, inc=1, device_id=where, device_id_type=MESH)

    loads = {}
    for q in range(CHUNKS):
        for side in range(2):
            at = (core if side == 0 else 1 - core) * CHUNKS + q
            span = pl.ds(pl.multiple_of(at * width, width), width)
            loads["in", q, side] = (
                pltpu.make_async_copy(gate_hbm.at[span, :], gate.at[at], w_sem.at[0, q, side]),
                pltpu.make_async_copy(up_hbm.at[span, :], up.at[at], w_sem.at[1, q, side]),
            )
            for copy in loads["in", q, side]:
                copy.start()
    for q in range(CHUNKS):
        for side in (1, 0):
            at = (core if side == 0 else 1 - core) * CHUNKS + q
            span = pl.ds(pl.multiple_of(at * width, width), width)
            loads["out", q, side] = pltpu.make_async_copy(down_hbm.at[:, span], down.at[at], w_sem.at[2, q, side])
            loads["out", q, side].start()

    for side in range(2):
        for q in range(CHUNKS):
            at = side * half + q * width
            piece = tokens[:, at : at + width].astype(F32)
            folded[side, q] = jnp.concatenate([piece[:, :fold], piece[:, fold:]], axis=0).astype(BF16)
    for q in range(CHUNKS):
        gathered[q, rank_rows(rank), :] = folded[core, q]

    diagonal = lax.broadcasted_iota(jnp.int32, (count, count), 0) == lax.broadcasted_iota(jnp.int32, (count, count), 1)

    def upright(line):
        return jnp.sum(jnp.where(diagonal, line, 0.0), axis=1, keepdims=True)

    first, second = upright(routes[0:1, :].astype(F32)), upright(routes[1:2, :].astype(F32))
    lanes = lax.broadcasted_iota(jnp.int32, (count, 128), 1)
    is_first = (lanes.astype(F32) == first).astype(F32)
    is_second = (lanes.astype(F32) == second).astype(F32)
    earlier = (
        lax.broadcasted_iota(jnp.int32, (count, count), 1) < lax.broadcasted_iota(jnp.int32, (count, count), 0)
    ).astype(F32)
    before = jnp.dot(earlier, is_first + is_second, preferred_element_type=F32)
    slot_first = jnp.sum(before * is_first, axis=1, keepdims=True)
    slot_second = jnp.sum((before + is_first) * is_second, axis=1, keepdims=True)
    base = (rank * capacity).astype(F32)
    row_first = first * block + base + slot_first
    row_second = second * block + base + slot_second
    facts = jnp.where(lanes == 2, upright(weights[0:1, :]), -1.0)
    facts = jnp.where(lanes == 3, upright(weights[1:2, :]), facts)
    upper = jnp.where(lanes == 0, row_first, jnp.where(lanes == 1, row_second, facts))
    lower = jnp.where(lanes == 4, row_first, jnp.where(lanes == 5, row_second, facts))
    meta[rank_rows(rank), :] = jnp.concatenate([upper, lower], axis=0)

    pl.semaphore_wait(barrier, len(rank_peers) + len(expert_peers))

    b_copies, bm_copies = {}, {}
    for d, where, there in rank_peers:
        part = meta.at[rank_rows(rank), :]
        bm_copies[d] = remote(part, part, bm_sem, (d - 1,), where)
        bm_copies[d].start()
    for q in range(CHUNKS):
        for d, where, there in rank_peers:
            b_copies[q, d] = remote(
                folded.at[lax.rem(there, 2), q], gathered.at[q, rank_rows(rank), :], b_sem, (q, d - 1), where
            )
            b_copies[q, d].start()
    for copy in bm_copies.values():
        copy.wait_recv()
    table = meta[...]
    turned = table.T
    row_ids = lax.broadcasted_iota(jnp.int32, (ranks * both, rows), 1).astype(F32)
    picks_left, picks_right = (
        jnp.concatenate([(row_ids == table[:, k : k + 1]).astype(BF16) for k in (n, n + 1)], axis=0) for n in (0, 4)
    )
    row_ids = lax.broadcasted_iota(jnp.int32, (rows, ranks * both), 0).astype(F32)
    place_left, place_right = (
        ((row_ids == turned[n : n + 1, :]).astype(F32) + (row_ids == turned[n + 1 : n + 2, :]).astype(F32)).astype(BF16)
        for n in (0, 4)
    )

    c_copies, d_copies = {}, {}
    for q in range(CHUNKS):
        for d, _, _ in rank_peers:
            b_copies[q, d].wait_recv()
        chosen_rows[q, :, :fold] = jnp.dot(place_left, gathered[q], preferred_element_type=F32).astype(BF16)
        chosen_rows[q, :, fold:] = jnp.dot(place_right, gathered[q], preferred_element_type=F32).astype(BF16)
        for d, where, there in expert_peers:
            c_copies[q, d] = remote(
                chosen_rows.at[q, block_rows(there), :], lhs.at[core, q, block_rows(expert), :],
                c_sem, (q, d - 1), where,
            )
            c_copies[q, d].start()
        lhs[core, q, block_rows(expert), :] = chosen_rows[q, block_rows(expert), :]
        part = lhs.at[core, q, block_rows(expert), :]
        d_copies[q, 0] = remote(part, part, d_sem, (q, 0), to_twin)
        d_copies[q, 0].start()

    unit_tile = tile_of(units, 512)

    def accumulate(q, side, fresh=False, last=False):
        at = core if side == 0 else 1 - core
        for copy in loads["in", q, side]:
            copy.wait()
        piece = at * CHUNKS + q

        def step(n, carry):
            span = pl.ds(pl.multiple_of(n * unit_tile, unit_tile), unit_tile)
            x = lhs[at, q]
            g = jnp.dot(x, gate[piece, :, span], preferred_element_type=F32)
            u = jnp.dot(x, up[piece, :, span], preferred_element_type=F32)
            if not fresh:
                g = g_acc[:, span] + g
                u = u_acc[:, span] + u
            if last:
                hidden[:, span] = (g / (1.0 + jnp.exp(-g)) * u).astype(BF16)
            else:
                g_acc[:, span] = g
                u_acc[:, span] = u
            return carry

        lax.fori_loop(0, units // unit_tile, step, 0)

    for q in range(CHUNKS):
        for d, _, _ in expert_peers:
            c_copies[q, d].wait_recv()
            part = lhs.at[core, q, block_rows(lax.rem(expert + groups - d, groups)), :]
            d_copies[q, d] = remote(part, part, d_sem, (q, d), to_twin)
            d_copies[q, d].start()
        accumulate(q, 0, fresh=q == 0)
        for d in range(groups):
            d_copies[q, d].wait_recv()
        accumulate(q, 1, last=q == CHUNKS - 1)

    out_tile = tile_of(width, 512)
    e_copies, f_copies = {}, {}

    def foreign(q):
        loads["out", q, 1].wait()

        def step(n, carry):
            span = pl.ds(pl.multiple_of(n * out_tile, out_tile), out_tile)
            half_send[q, :, span] = jnp.dot(
                hidden[...], down[(1 - core) * CHUNKS + q, :, span], preferred_element_type=F32
            ).astype(BF16)
            return carry

        lax.fori_loop(0, width // out_tile, step, 0)
        e_copies[q] = remote(half_send.at[q], half_recv.at[q], e_sem, (q,), to_twin)
        e_copies[q].start()

    def native(q):
        loads["out", q, 0].wait()
        e_copies[q].wait_recv()

        def step(n, carry):
            span = pl.ds(pl.multiple_of(n * out_tile, out_tile), out_tile)
            part = jnp.dot(hidden[...], down[core * CHUNKS + q, :, span], preferred_element_type=F32)
            summed[q, :, span] = (part + half_recv[q, :, span].astype(F32)).astype(BF16)
            return carry

        lax.fori_loop(0, width // out_tile, step, 0)
        for d, where, there in expert_peers:
            f_copies[q, d] = remote(
                summed.at[q, block_rows(there), :], returned.at[q, block_rows(expert), :], f_sem, (q, d - 1), where
            )
            f_copies[q, d].start()
        returned[q, block_rows(expert), :] = summed[q, block_rows(expert), :]

    foreign(0)
    for q in range(CHUNKS):
        if q + 1 < CHUNKS:
            foreign(q + 1)
        native(q)

    g_copies = {}
    folded_rows = ranks * both
    for q in range(CHUNKS):
        for d, _, _ in expert_peers:
            f_copies[q, d].wait_recv()
        picked = jnp.dot(picks_left, returned[q, :, :fold], preferred_element_type=F32) + jnp.dot(
            picks_right, returned[q, :, fold:], preferred_element_type=F32
        )
        mixture = table[:, 2:3] * picked[:folded_rows] + table[:, 3:4] * picked[folded_rows:]
        mixed_send[q] = mixture.astype(BF16)
        for d, where, there in rank_peers:
            g_copies[q, d] = remote(
                mixed_send.at[q, rank_rows(there), :], mixed_recv.at[q, rank_rows(rank), :], g_sem, (q, d - 1), where
            )
            g_copies[q, d].start()
        mixed_recv[q, rank_rows(rank), :] = mixed_send[q, rank_rows(rank), :]

    for q in range(CHUNKS):
        for d, _, _ in rank_peers:
            g_copies[q, d].wait_recv()
        for side in range(2):
            total = mixed_recv[q, side * both : (side + 1) * both, :].astype(F32)
            for r in range(side + 2, ranks, 2):
                total = total + mixed_recv[q, r * both : (r + 1) * both, :].astype(F32)
            at = side * half + q * width
            out[:, at : at + fold] = total[:count].astype(BF16)
            out[:, at + fold : at + width] = total[count:].astype(BF16)

    for copies in (bm_copies, b_copies, c_copies, d_copies, e_copies, f_copies, g_copies):
        for copy in copies.values():
            copy.wait_send()


def local(tokens, routes, route_weights, w_gate, w_up, w_down):
    groups, ranks = lax.axis_size("expert"), lax.axis_size("dp")
    count, features = tokens.shape
    units = w_gate.shape[2]
    capacity = 3 * count // groups
    block = -(-(ranks * capacity) // 16) * 16
    rows = groups * block
    half = features // 2
    width = half // CHUNKS
    both = 2 * count
    dma = pltpu.SemaphoreType.DMA
    return pl.pallas_call(
        functools.partial(kernel, groups, ranks, capacity, block),
        out_shape=jax.ShapeDtypeStruct((count, features), BF16),
        in_specs=[pl.BlockSpec(memory_space=pltpu.VMEM)] * 3 + [pl.BlockSpec(memory_space=pl.ANY)] * 3,
        out_specs=pl.BlockSpec(memory_space=pltpu.VMEM),
        scratch_shapes=[
            pltpu.VMEM((2 * CHUNKS, width, units), BF16),
            pltpu.VMEM((2 * CHUNKS, width, units), BF16),
            pltpu.VMEM((2 * CHUNKS, units, width), BF16),
            dma((3, CHUNKS, 2)),
            pltpu.VMEM((2, CHUNKS, both, width // 2), BF16),
            pltpu.VMEM((ranks * both, 128), F32),
            pltpu.VMEM((CHUNKS, ranks * both, width // 2), BF16),
            pltpu.VMEM((CHUNKS, rows, width), BF16),
            pltpu.VMEM((2, CHUNKS, rows, width), BF16),
            pltpu.VMEM((rows, units), F32),
            pltpu.VMEM((rows, units), F32),
            pltpu.VMEM((rows, units), BF16),
            pltpu.VMEM((CHUNKS, rows, width), BF16),
            pltpu.VMEM((CHUNKS, rows, width), BF16),
            pltpu.VMEM((CHUNKS, rows, width), BF16),
            pltpu.VMEM((CHUNKS, rows, width), BF16),
            pltpu.VMEM((CHUNKS, ranks * both, width // 2), BF16),
            pltpu.VMEM((CHUNKS, ranks * both, width // 2), BF16),
            dma((2, CHUNKS, ranks - 1)),
            dma((2, ranks - 1)),
            dma((2, CHUNKS, groups - 1)),
            dma((2, CHUNKS, groups)),
            dma((2, CHUNKS)),
            dma((2, CHUNKS, groups - 1)),
            dma((2, CHUNKS, ranks - 1)),
        ],
        compiler_params=pltpu.CompilerParams(
            collective_id=0, has_side_effects=True, vmem_limit_bytes=60 * 1024 * 1024
        ),
        cost_estimate=pl.CostEstimate(
            flops=6 * rows * features * units, bytes_accessed=6 * features * units, transcendentals=rows * units
        ),
    )(tokens, routes.T, route_weights.T, w_gate[0], w_up[0], w_down[0])


def solution(mesh):
    placed = (
        P(("expert", "dp"), None),
        P(("expert", "dp"), None),
        P(("expert", "dp"), None),
        P("expert", None, "dp"),
        P("expert", None, "dp"),
        P("expert", "dp", None),
    )
    return jax.shard_map(
        local, mesh=mesh, in_specs=placed, out_specs=P(("expert", "dp"), None), check_vma=False
    )
```

time: 56.1 us -> 53.3 us (0.950)
  local copies, waits for them, and re-layouts: 4.16 us -> 1.47 us
    unnamed x3 -> x1, local copies, waits for them, and re-layouts: 4.16 us -> 1.47 us
where the time goes in v2:
time: 53.3 us; the launch traced here: 53.1 us
  Pallas kernels  51.6 us (97%)
  local copies, waits for them, and re-layouts  1.47 us (3%)
    pallas_call x1, Pallas kernels, local(): pl.pallas_call(functools.partial(kernel, groups, ranks, capacity, block),...  51.6 us
    unnamed x1, local copies, waits for them, and re-layouts  1.47 us

profile of v2, /device:TPU:0, one launch (start us, length us, event | category | flops | bytes accessed | tf_op | source)
XLA Modules:
  0.0 53.1 jit_solution(10708470732272556179)
XLA Ops:
  0.0 51.6 %shard_map.64 = bf16[8,4096]{1,0:T(8,128)(2,1)} custom-call(bf16[8,4096]{1,0:T(8,128)(2,1)} %tokens.1, s32[2,8]{1,0:T(2,128)} %bitcast.8, f32[2,8]{1,0:T(2,128)} %bitcast.9, bf16[4096,1792]{1,0:T(8,128)(2,1)} %bitcast.5, bf16[4096,1792]{1,0:T(8,128)(2,1)} %bitcast.6, bf16[1792,4096]{1,0:T(8,128)(2,1)} %bitcast.7), custom_call_target="tpu_custom_call" | custom-call | flops 8455716864 | bytes 44040192 | tf_op jit(solution)/shard_map/pallas_call | solution.py:275
  51.6 1.5 %copy.8 = bf16[8,4096]{1,0:T(8,128)(2,1)} copy(bf16[8,4096]{1,0:T(8,128)(2,1)} %shard_map.64) | data formatting | bytes 131072

commit v3 on v2

--- a/solution.py
+++ b/solution.py
@@ -11,6 +11,8 @@
 BF16 = jnp.bfloat16
 F32 = jnp.float32
 CHUNKS = 4
+TOKEN_GROUPS = ((0, 1), (1, 3))
+RESULT_GROUPS = ((0, 2), (2, 1), (3, 1))
 
 
 def tile_of(extent, most):
@@ -114,10 +116,11 @@
         part = meta.at[rank_rows(rank), :]
         bm_copies[d] = remote(part, part, bm_sem, (d - 1,), where)
         bm_copies[d].start()
-    for q in range(CHUNKS):
+    for q, n in TOKEN_GROUPS:
         for d, where, there in rank_peers:
             b_copies[q, d] = remote(
-                folded.at[lax.rem(there, 2), q], gathered.at[q, rank_rows(rank), :], b_sem, (q, d - 1), where
+                folded.at[lax.rem(there, 2), pl.ds(q, n)], gathered.at[pl.ds(q, n), rank_rows(rank), :],
+                b_sem, (q, d - 1), where,
             )
             b_copies[q, d].start()
     for copy in bm_copies.values():
@@ -137,7 +140,8 @@
     c_copies, d_copies = {}, {}
     for q in range(CHUNKS):
         for d, _, _ in rank_peers:
-            b_copies[q, d].wait_recv()
+            if (q, d) in b_copies:
+                b_copies[q, d].wait_recv()
         chosen_rows[q, :, :fold] = jnp.dot(place_left, gathered[q], preferred_element_type=F32).astype(BF16)
         chosen_rows[q, :, fold:] = jnp.dot(place_right, gathered[q], preferred_element_type=F32).astype(BF16)
         for d, where, there in expert_peers:
@@ -151,7 +155,7 @@
         d_copies[q, 0] = remote(part, part, d_sem, (q, 0), to_twin)
         d_copies[q, 0].start()
 
-    unit_tile = tile_of(units, 512)
+    unit_tile = tile_of(units, 256)
 
     def accumulate(q, side, fresh=False, last=False):
         at = core if side == 0 else 1 - core
@@ -174,7 +178,7 @@
                 u_acc[:, span] = u
             return carry
 
-        lax.fori_loop(0, units // unit_tile, step, 0)
+        lax.fori_loop(0, units // unit_tile, step, 0, unroll=True)
 
     for q in range(CHUNKS):
         for d, _, _ in expert_peers:
@@ -187,7 +191,7 @@
             d_copies[q, d].wait_recv()
         accumulate(q, 1, last=q == CHUNKS - 1)
 
-    out_tile = tile_of(width, 512)
+    out_tile = tile_of(width, 256)
     e_copies, f_copies = {}, {}
 
     def foreign(q):
@@ -200,7 +204,7 @@
             ).astype(BF16)
             return carry
 
-        lax.fori_loop(0, width // out_tile, step, 0)
+        lax.fori_loop(0, width // out_tile, step, 0, unroll=True)
         e_copies[q] = remote(half_send.at[q], half_recv.at[q], e_sem, (q,), to_twin)
         e_copies[q].start()
 
@@ -214,7 +218,7 @@
             summed[q, :, span] = (part + half_recv[q, :, span].astype(F32)).astype(BF16)
             return carry
 
-        lax.fori_loop(0, width // out_tile, step, 0)
+        lax.fori_loop(0, width // out_tile, step, 0, unroll=True)
         for d, where, there in expert_peers:
             f_copies[q, d] = remote(
                 summed.at[q, block_rows(there), :], returned.at[q, block_rows(expert), :], f_sem, (q, d - 1), where
@@ -228,8 +232,12 @@
             foreign(q + 1)
         native(q)
 
+    for copies in (bm_copies, b_copies, c_copies, d_copies, e_copies):
+        for copy in copies.values():
+            copy.wait_send()
     g_copies = {}
     folded_rows = ranks * both
+    ready = {q + n - 1: (q, n) for q, n in RESULT_GROUPS}
     for q in range(CHUNKS):
         for d, _, _ in expert_peers:
             f_copies[q, d].wait_recv()
@@ -238,16 +246,23 @@
         )
         mixture = table[:, 2:3] * picked[:folded_rows] + table[:, 3:4] * picked[folded_rows:]
         mixed_send[q] = mixture.astype(BF16)
+        mixed_recv[q, rank_rows(rank), :] = mixed_send[q, rank_rows(rank), :]
+        if q not in ready:
+            continue
+        at, n = ready[q]
         for d, where, there in rank_peers:
-            g_copies[q, d] = remote(
-                mixed_send.at[q, rank_rows(there), :], mixed_recv.at[q, rank_rows(rank), :], g_sem, (q, d - 1), where
-            )
-            g_copies[q, d].start()
-        mixed_recv[q, rank_rows(rank), :] = mixed_send[q, rank_rows(rank), :]
-
+            g_copies[at, d] = remote(
+                mixed_send.at[pl.ds(at, n), rank_rows(there), :], mixed_recv.at[pl.ds(at, n), rank_rows(rank), :],
+                g_sem, (at, d - 1), where,
+            )
+            g_copies[at, d].start()
+
+    for copy in f_copies.values():
+        copy.wait_send()
     for q in range(CHUNKS):
         for d, _, _ in rank_peers:
-            g_copies[q, d].wait_recv()
+            if (q, d) in g_copies:
+                g_copies[q, d].wait_recv()
         for side in range(2):
             total = mixed_recv[q, side * both : (side + 1) * both, :].astype(F32)
             for r in range(side + 2, ranks, 2):
@@ -256,9 +271,8 @@
             out[:, at : at + fold] = total[:count].astype(BF16)
             out[:, at + fold : at + width] = total[count:].astype(BF16)
 
-    for copies in (bm_copies, b_copies, c_copies, d_copies, e_copies, f_copies, g_copies):
-        for copy in copies.values():
-            copy.wait_send()
+    for copy in g_copies.values():
+        copy.wait_send()
 
 
 def local(tokens, routes, route_weights, w_gate, w_up, w_down):

time: 53.3 us -> 47.7 us (0.89)
  Pallas kernels: 51.6 us -> 46 us
    pallas_call x1, Pallas kernels: 51.6 us -> 46 us  [local(): pl.pallas_call(functools.partial(kernel, groups, ranks, capacity, block),...]
where the time goes in v3:
time: 47.7 us; the launch traced here: 47.5 us
  Pallas kernels  46 us (96%)
  local copies, waits for them, and re-layouts  1.47 us (3%)
    pallas_call x1, Pallas kernels, local(): pl.pallas_call(functools.partial(kernel, groups, ranks, capacity, block),...  46 us
    unnamed x1, local copies, waits for them, and re-layouts  1.47 us

profile of v3, /device:TPU:0, one launch (start us, length us, event | category | flops | bytes accessed | tf_op | source)
XLA Modules:
  0.0 47.5 jit_solution(14477625037419633709)
XLA Ops:
  0.0 46.0 %shard_map.64 = bf16[8,4096]{1,0:T(8,128)(2,1)} custom-call(bf16[8,4096]{1,0:T(8,128)(2,1)} %tokens.1, s32[2,8]{1,0:T(2,128)} %bitcast.8, f32[2,8]{1,0:T(2,128)} %bitcast.9, bf16[4096,1792]{1,0:T(8,128)(2,1)} %bitcast.5, bf16[4096,1792]{1,0:T(8,128)(2,1)} %bitcast.6, bf16[1792,4096]{1,0:T(8,128)(2,1)} %bitcast.7), custom_call_target="tpu_custom_call" | custom-call | flops 8455716864 | bytes 44040192 | tf_op jit(solution)/shard_map/pallas_call | solution.py:289
  46.0 1.5 %copy.8 = bf16[8,4096]{1,0:T(8,128)(2,1)} copy(bf16[8,4096]{1,0:T(8,128)(2,1)} %shard_map.64) | data formatting | bytes 131072

commit v4 on v3

--- a/solution.py
+++ b/solution.py
@@ -15,8 +15,8 @@
 RESULT_GROUPS = ((0, 2), (2, 1), (3, 1))
 
 
-def tile_of(extent, most):
-    return max([t for t in range(128, most + 1, 128) if extent % t == 0], default=extent)
+def tiles_of(extent, most=512):
+    return [slice(at, min(at + most, extent)) for at in range(0, extent, most)]
 
 
 def kernel(
@@ -155,16 +155,13 @@
         d_copies[q, 0] = remote(part, part, d_sem, (q, 0), to_twin)
         d_copies[q, 0].start()
 
-    unit_tile = tile_of(units, 256)
-
     def accumulate(q, side, fresh=False, last=False):
         at = core if side == 0 else 1 - core
         for copy in loads["in", q, side]:
             copy.wait()
         piece = at * CHUNKS + q
 
-        def step(n, carry):
-            span = pl.ds(pl.multiple_of(n * unit_tile, unit_tile), unit_tile)
+        for span in tiles_of(units):
             x = lhs[at, q]
             g = jnp.dot(x, gate[piece, :, span], preferred_element_type=F32)
             u = jnp.dot(x, up[piece, :, span], preferred_element_type=F32)
@@ -176,9 +173,6 @@
             else:
                 g_acc[:, span] = g
                 u_acc[:, span] = u
-            return carry
-
-        lax.fori_loop(0, units // unit_tile, step, 0, unroll=True)
 
     for q in range(CHUNKS):
         for d, _, _ in expert_peers:
@@ -191,34 +185,25 @@
             d_copies[q, d].wait_recv()
         accumulate(q, 1, last=q == CHUNKS - 1)
 
-    out_tile = tile_of(width, 256)
     e_copies, f_copies = {}, {}
 
     def foreign(q):
         loads["out", q, 1].wait()
-
-        def step(n, carry):
-            span = pl.ds(pl.multiple_of(n * out_tile, out_tile), out_tile)
+        piece = (1 - core) * CHUNKS + q
+        for span in tiles_of(width):
             half_send[q, :, span] = jnp.dot(
-                hidden[...], down[(1 - core) * CHUNKS + q, :, span], preferred_element_type=F32
+                hidden[...], down[piece, :, span], preferred_element_type=F32
             ).astype(BF16)
-            return carry
-
-        lax.fori_loop(0, width // out_tile, step, 0, unroll=True)
         e_copies[q] = remote(half_send.at[q], half_recv.at[q], e_sem, (q,), to_twin)
         e_copies[q].start()
 
     def native(q):
         loads["out", q, 0].wait()
+        piece = core * CHUNKS + q
+        parts = [jnp.dot(hidden[...], down[piece, :, span], preferred_element_type=F32) for span in tiles_of(width)]
         e_copies[q].wait_recv()
-
-        def step(n, carry):
-            span = pl.ds(pl.multiple_of(n * out_tile, out_tile), out_tile)
-            part = jnp.dot(hidden[...], down[core * CHUNKS + q, :, span], preferred_element_type=F32)
+        for part, span in zip(parts, tiles_of(width)):
             summed[q, :, span] = (part + half_recv[q, :, span].astype(F32)).astype(BF16)
-            return carry
-
-        lax.fori_loop(0, width // out_tile, step, 0, unroll=True)
         for d, where, there in expert_peers:
             f_copies[q, d] = remote(
                 summed.at[q, block_rows(there), :], returned.at[q, block_rows(expert), :], f_sem, (q, d - 1), where
@@ -227,7 +212,9 @@
         returned[q, block_rows(expert), :] = summed[q, block_rows(expert), :]
 
     foreign(0)
-    for q in range(CHUNKS):
+    native(0)
+    foreign(1)
+    for q in range(1, CHUNKS):
         if q + 1 < CHUNKS:
             foreign(q + 1)
         native(q)

time: 47.7 us -> 47.7 us (level)
  no operation moved by 1% of the time
where the time goes in v4:
time: 47.7 us; the launch traced here: 47.5 us
  Pallas kernels  46 us (96%)
  local copies, waits for them, and re-layouts  1.47 us (3%)
    pallas_call x1, Pallas kernels, local(): pl.pallas_call(functools.partial(kernel, groups, ranks, capacity, block),...  46 us
    unnamed x1, local copies, waits for them, and re-layouts  1.47 us

profile of v4, /device:TPU:0, one launch (start us, length us, event | category | flops | bytes accessed | tf_op | source)
XLA Modules:
  0.0 47.5 jit_solution(9501958220785752171)
XLA Ops:
  0.0 46.0 %shard_map.64 = bf16[8,4096]{1,0:T(8,128)(2,1)} custom-call(bf16[8,4096]{1,0:T(8,128)(2,1)} %tokens.1, s32[2,8]{1,0:T(2,128)} %bitcast.8, f32[2,8]{1,0:T(2,128)} %bitcast.9, bf16[4096,1792]{1,0:T(8,128)(2,1)} %bitcast.5, bf16[4096,1792]{1,0:T(8,128)(2,1)} %bitcast.6, bf16[1792,4096]{1,0:T(8,128)(2,1)} %bitcast.7), custom_call_target="tpu_custom_call" | custom-call | flops 8455716864 | bytes 44040192 | tf_op jit(solution)/shard_map/pallas_call | solution.py:276
  46.0 1.5 %copy.8 = bf16[8,4096]{1,0:T(8,128)(2,1)} copy(bf16[8,4096]{1,0:T(8,128)(2,1)} %shard_map.64) | data formatting | bytes 131072

commit v5 on v3

--- a/solution.py
+++ b/solution.py
@@ -60,7 +60,8 @@
         pl.semaphore_signal(barrier, inc=1, device_id=where, device_id_type=MESH)
 
     loads = {}
-    for q in range(CHUNKS):
+
+    def load_in(q):
         for side in range(2):
             at = (core if side == 0 else 1 - core) * CHUNKS + q
             span = pl.ds(pl.multiple_of(at * width, width), width)
@@ -70,12 +71,15 @@
             )
             for copy in loads["in", q, side]:
                 copy.start()
-    for q in range(CHUNKS):
+
+    def load_out(q):
         for side in (1, 0):
             at = (core if side == 0 else 1 - core) * CHUNKS + q
             span = pl.ds(pl.multiple_of(at * width, width), width)
             loads["out", q, side] = pltpu.make_async_copy(down_hbm.at[:, span], down.at[at], w_sem.at[2, q, side])
             loads["out", q, side].start()
+
+    load_in(0)
 
     for side in range(2):
         for q in range(CHUNKS):
@@ -123,6 +127,7 @@
                 b_sem, (q, d - 1), where,
             )
             b_copies[q, d].start()
+    load_in(1)
     for copy in bm_copies.values():
         copy.wait_recv()
     table = meta[...]
@@ -154,6 +159,10 @@
         part = lhs.at[core, q, block_rows(expert), :]
         d_copies[q, 0] = remote(part, part, d_sem, (q, 0), to_twin)
         d_copies[q, 0].start()
+        if q == 0:
+            load_in(2)
+    for q in range(3, CHUNKS):
+        load_in(q)
 
     unit_tile = tile_of(units, 256)
 
@@ -186,6 +195,7 @@
             part = lhs.at[core, q, block_rows(lax.rem(expert + groups - d, groups)), :]
             d_copies[q, d] = remote(part, part, d_sem, (q, d), to_twin)
             d_copies[q, d].start()
+        load_out(q)
         accumulate(q, 0, fresh=q == 0)
         for d in range(groups):
             d_copies[q, d].wait_recv()

time: 47.7 us -> 47.7 us (level)
  no operation moved by 1% of the time
where the time goes in v5:
time: 47.7 us; the launch traced here: 47.5 us
  Pallas kernels  46 us (96%)
  local copies, waits for them, and re-layouts  1.47 us (3%)
    pallas_call x1, Pallas kernels, local(): pl.pallas_call(functools.partial(kernel, groups, ranks, capacity, block),...  46 us
    unnamed x1, local copies, waits for them, and re-layouts  1.47 us

profile of v5, /device:TPU:0, one launch (start us, length us, event | category | flops | bytes accessed | tf_op | source)
XLA Modules:
  0.0 47.5 jit_solution(18166539170024271136)
XLA Ops:
  0.0 46.0 %shard_map.64 = bf16[8,4096]{1,0:T(8,128)(2,1)} custom-call(bf16[8,4096]{1,0:T(8,128)(2,1)} %tokens.1, s32[2,8]{1,0:T(2,128)} %bitcast.8, f32[2,8]{1,0:T(2,128)} %bitcast.9, bf16[4096,1792]{1,0:T(8,128)(2,1)} %bitcast.5, bf16[4096,1792]{1,0:T(8,128)(2,1)} %bitcast.6, bf16[1792,4096]{1,0:T(8,128)(2,1)} %bitcast.7), custom_call_target="tpu_custom_call" | custom-call | flops 8455716864 | bytes 44040192 | tf_op jit(solution)/shard_map/pallas_call | solution.py:299
  46.0 1.5 %copy.8 = bf16[8,4096]{1,0:T(8,128)(2,1)} copy(bf16[8,4096]{1,0:T(8,128)(2,1)} %shard_map.64) | data formatting | bytes 131072
